TPU v7x, 32 devices: a whole 2x2x4 slice. The times are simulated.
32 devices in a mesh: grp: 2 (over y), bond: 4 (over z), mpo: 2 (over x), sub: 2 (over core).
Axes of the slice: x: 2, y: 2, z: 4, core: 2. Of those that a mesh axis runs over, the one named last changes fastest.
Arguments:
- psi: bfloat16 [2, 192, 128, 128], P(None, ('grp', 'bond'), 'sub'), parts along dimension 1, may hold values from -6 to 6
- left_env: bfloat16 [40, 64, 128, 128], P('mpo', ('grp', 'bond')), parts along dimension 1, may hold values from -0.078125 to 0.078125
- right_env: bfloat16 [40, 64, 128, 128], P('mpo', ('grp', 'bond'), 'sub'), parts along dimension 1, may hold values from -0.5 to 0.5
- left_sector: int32 [192], P(('grp', 'bond')), parts along dimension 0, may hold values from 0 to 7
- right_sector: int32 [192], P(('grp', 'bond')), parts along dimension 0, may hold values from 0 to 7
- dest_device: int32 [192, 1], P(('grp', 'bond')), parts along dimension 0, may hold values from 0 to 3; in each aligned block of 24 rows (0 to 23, 24 to 47, ...) at most 12 rows name the same one
- target_block: int32 [192], P(('grp', 'bond')), parts along dimension 0, may hold values from 0 to 23
- left_size: int32 [64], P(('grp', 'bond')), parts along dimension 0, may hold values from 1 to 128
- right_size: int32 [64], P(('grp', 'bond')), parts along dimension 0, may hold values from 1 to 128
Outputs:
- h_psi: bfloat16 [2, 192, 128, 128], P(None, ('grp', 'bond'), ('mpo', 'sub')), parts along dimension 1
There are 2 independent parts, one for each index of `grp`. A program takes and returns all parts, laid end to end along the dimension named above; each array names one. Nothing has to cross between parts.
Inputs may be any that keep to these rules, and one draw needn't show every extreme that they name: Local indices: left_sector into the sectors of the block's own index of bond, right_sector and target_block into those of its destination. `dest_device`: among the 24 blocks of one index of bond no destination occurs more than 12 times, and some destination occurs exactly 12 times.
All inputs are finite; a program needn't handle non-finite values.
Results may differ from a plain program's by a relative error of at most 0.0049.
Values may be sent and summed in bfloat16 or wider, within the bound.
A program may use at most 256 MiB of HBM per device.

v0:
```python
import jax
import jax.numpy as jnp
from jax import lax
from jax.sharding import PartitionSpec as P


def body(
    psi,
    left_env,
    right_env,
    left_sector,
    right_sector,
    dest_device,
    target_block,
    left_size,
    right_size,
):
    blocks = psi.shape[1]
    width = psi.shape[2]
    states = psi.shape[3]
    peers = lax.axis_size("bond")
    capacity = max(2, 2 * blocks // peers)
    slots = peers * capacity
    rows_all = jnp.arange(states, dtype=jnp.int32)
    left_in = rows_all[None, :] < left_size[:, None]
    masked_left = jnp.where(
        left_in[None, :, :, None] & left_in[None, :, None, :], left_env, jnp.zeros_like(left_env)
    )
    col_rows = lax.axis_index("sub") * width + jnp.arange(width, dtype=jnp.int32)
    right_rows = col_rows[None, :] < right_size[:, None]
    right_cols = rows_all[None, :] < right_size[:, None]
    masked_right = jnp.where(
        right_rows[None, :, :, None] & right_cols[None, :, None, :],
        right_env,
        jnp.zeros_like(right_env),
    )
    left_pieces = masked_left[:, left_sector]
    destination = dest_device[:, 0]
    peer_hits = (destination[:, None] == jnp.arange(peers, dtype=jnp.int32)[None, :]).astype(
        jnp.int32
    )
    earlier = jnp.sum(peer_hits * (jnp.cumsum(peer_hits, axis=0) - peer_hits), axis=1)
    slot_of = destination * capacity + earlier
    block_ids = jnp.arange(blocks, dtype=jnp.int32)
    labels = (
        jnp.zeros((slots, 2), jnp.int32)
        .at[slot_of]
        .set(jnp.stack([target_block, right_sector], axis=1))
    )
    half = jnp.einsum(
        "vkcb,wkab->kvwca", psi, left_pieces, preferred_element_type=jnp.float32
    ).astype(jnp.bfloat16)
    empty = jnp.zeros((slots,) + half.shape[1:], jnp.bfloat16)
    received = lax.all_to_all(
        empty.at[slot_of].set(half), "bond", split_axis=0, concat_axis=0, tiled=True
    )
    labels_in = lax.all_to_all(labels, "bond", split_axis=0, concat_axis=0, tiled=True)
    right_pieces = masked_right[:, labels_in[:, 1]]
    product = jnp.einsum(
        "jvwca,wjcd->vjad", received, right_pieces, preferred_element_type=jnp.float32
    )
    placing = (labels_in[:, 0][:, None] == block_ids[None, :]).astype(jnp.float32)
    partial_sum = jnp.einsum("jt,vjad->vtad", placing, product, precision=lax.Precision.HIGHEST)
    return lax.psum_scatter(partial_sum, ("mpo", "sub"), scatter_dimension=2, tiled=True).astype(
        jnp.bfloat16
    )


def solution(mesh):
    in_specs = (
        P(None, ("grp", "bond"), "sub", None),
        P("mpo", ("grp", "bond"), None, None),
        P("mpo", ("grp", "bond"), "sub", None),
        P(("grp", "bond")),
        P(("grp", "bond")),
        P(("grp", "bond"), None),
        P(("grp", "bond")),
        P(("grp", "bond")),
        P(("grp", "bond")),
    )
    out_specs = P(None, ("grp", "bond"), ("mpo", "sub"), None)
    return jax.shard_map(body, mesh=mesh, in_specs=in_specs, out_specs=out_specs, check_vma=False)
```

profile of v0, /device:TPU:0, one launch (start us, length us, event | category | flops | bytes accessed | tf_op | source)
XLA Modules:
  0.0 860.7 jit_solution(15362218015424864391)
XLA Ops:
  6.5 0.0 copy-start
  6.5 0.8 fusion.10
  7.4 0.8 select_reduce_fusion
  8.2 0.7 fusion.16
  8.9 0.7 pad_add_fusion
  9.6 0.1 copy.14
  9.7 0.7 scatter_custom_fusion
  10.3 0.1 copy.15
  10.4 0.1 all_to_all.11
  10.5 0.6 copy.16
  11.1 6.3 all-to-all-start
  17.4 0.7 iota_compare_fusion.2
  18.1 0.2 broadcast_and_fusion
  18.3 0.7 compare_select_fusion
  19.0 5.5 broadcast_select_fusion
  24.5 9.7 %gather_fusion.1 = bf16[24,20,128,128]{3,2,1,0:T(8,128)(2,1)} fusion(bf16[20,8,128,128]{3,2,1,0:T(8,128)(2,1)} %broadcast_select_fusion, s32[1024]{0:T(1024)S(1)} %pad_clamp_fusion), kind=kCustom, calls=%fused_computation.1 | custom fusion | bytes 31457376 | tf_op jit(solution)/shard_map/gather | solution.py:37
  34.2 0.0 copy-done
  34.2 14.0 %convert_bitcast_fusion = bf16[24,2,20,64,128]{4,3,2,1,0:T(8,128)(2,1)} fusion(bf16[24,20,128,128]{3,2,1,0:T(8,128)(2,1)} %gather_fusion.1, bf16[2,24,64,128]{3,2,1,0:T(8,128)(2,1)S(1)} %copy-done), kind=kOutput, calls=%fused_computation.8 | convolution fusion | flops 2021130240 | bytes 32243712 | tf_op jit(solution)/shard_map/vkcb,wkab->kvwca/dot_general | solution.py:50
  48.2 10.6 %broadcast_in_dim.29 = bf16[48,2,20,64,128]{4,3,2,1,0:T(8,128)(2,1)} broadcast(bf16[]{:T(256)} %constant.9.clone.1), dimensions={} | broadcast | bytes 31457282 | tf_op jit(solution)/shard_map/broadcast_in_dim | solution.py:53
  58.9 35.0 %scatter_fusion = bf16[48,2,20,64,128]{4,3,2,1,0:T(8,128)(2,1)} fusion(bf16[48,2,20,64,128]{4,3,2,1,0:T(8,128)(2,1)} %broadcast_in_dim.29, s32[24]{0:T(128)S(1)} %fusion.16, bf16[24,2,20,64,128]{4,3,2,1,0:T(8,128)(2,1)} %convert_bitcast_fusion), kind=kCustom, calls=%fused_computation.3 | custom fusion | bytes 47186016 | tf_op jit(solution)/shard_map/scatter | solution.py:55
  93.8 0.0 copy-start.2
  93.8 0.0 all-to-all-done
  93.8 9.5 %all-to-all-start.1 = ((bf16[48,2,20,64,128]{4,3,2,1,0:T(8,128)(2,1)}), bf16[48,2,20,64,128]{4,3,2,1,0:T(8,128)(2,1)}, u32[]{:S(2)}, u32[]{:S(2)}) async-start(bf16[48,2,20,64,128]{4,3,2,1,0:T(8,128)(2,1)} %scatter_fusion), calls=%async_computation.1 | async-start | bytes 62914560 | tf_op jit(solution)/shard_map/all_to_all | solution.py:54
  103.4 0.0 reduce-scatter.5.cloned.1.call-start
  103.4 0.0 copy-done.2
  103.5 0.1 iota_compare_fusion.3
  103.5 0.1 broadcast_compare_fusion
  103.6 0.1 broadcast_and_fusion.1
  103.7 1.9 broadcast_select_fusion.1
  105.7 0.1 all_to_all.13
  105.8 7.4 gather_fusion
  113.2 667.7 %all-to-all-done.1 = bf16[48,2,20,64,128]{4,3,2,1,0:T(8,128)(2,1)} async-done(((bf16[48,2,20,64,128]{4,3,2,1,0:T(8,128)(2,1)}), bf16[48,2,20,64,128]{4,3,2,1,0:T(8,128)(2,1)}, u32[]{:S(2)}, u32[]{:S(2)}) %all-to-all-start.1) | async-done | bytes 31457312 | tf_op jit(solution)/shard_map/all_to_all | solution.py:54
  780.9 19.6 %fusion.6 = f32[2,48,128,128]{2,3,0,1:T(8,128)} fusion(bf16[48,2,20,64,128]{4,3,2,1,0:T(8,128)(2,1)} %all-to-all-done.1, bf16[48,20,64,128]{3,2,1,0:T(8,128)(2,1)} %gather_fusion), kind=kOutput, calls=%fused_computation.11 | convolution fusion | flops 4026531840 | bytes 53477376 | tf_op jit(solution)/shard_map/jvwca,wjcd->vjad/dot_general | solution.py:59
  800.5 0.0 copy-start.1
  800.5 6.7 copy.19
  807.2 4.4 convolution_bitcast_fusion
  811.6 0.2 copy.28
  811.8 2.7 copy.37
  814.5 0.0 reduce-scatter.5.cloned.1.call-update
  814.5 37.2 %reduce-scatter.5.cloned.1.call-done = f32[32,6144]{1,0:T(8,128)} async-done(((f32[128,6144]{1,0:T(8,128)}), f32[32,6144]{1,0:T(8,128)}) %reduce-scatter.5.cloned.1.call-update) | async-done | bytes 786448
  851.7 1.3 copy.31
  853.1 0.8 copy.20
  853.9 0.0 copy-done.1
  (7 shorter events, 0.1 us)
Async XLA Ops:
  6.5 27.7 %copy-start = (bf16[2,24,64,128]{3,2,1,0:T(8,128)(2,1)S(1)}, bf16[2,24,64,128]{3,2,1,0:T(8,128)(2,1)}, u32[]{:S(2)}) copy-start(bf16[2,24,64,128]{3,2,1,0:T(8,128)(2,1)} %param.9) | copy-start | bytes 2359300
  11.1 82.8 %all-to-all-start = ((s32[4,12,2]{1,2,0:T(2,128)}), s32[4,12,2]{1,2,0:T(2,128)S(1)}, u32[]{:S(2)}, u32[]{:S(2)}) async-start(s32[4,12,2]{1,2,0:T(2,128)} %copy.16), calls=%async_computation | async-start | bytes 8192 | tf_op jit(solution)/shard_map/all_to_all | solution.py:57
  93.8 9.6 %copy-start.2 = (s32[8]{0:T(128)S(1)}, s32[8]{0:T(128)}, u32[]{:S(2)}) copy-start(s32[8]{0:T(128)} %param.17) | copy-start | bytes 100
  93.8 687.1 %all-to-all-start.1 = ((bf16[48,2,20,64,128]{4,3,2,1,0:T(8,128)(2,1)}), bf16[48,2,20,64,128]{4,3,2,1,0:T(8,128)(2,1)}, u32[]{:S(2)}, u32[]{:S(2)}) async-start(bf16[48,2,20,64,128]{4,3,2,1,0:T(8,128)(2,1)} %scatter_fusion), calls=%async_computation.1 | async-start | bytes 62914560 | tf_op jit(solution)/shard_map/all_to_all | solution.py:54
  103.4 748.4 %reduce-scatter.5.cloned.1.call-start = ((), (), s32[]{:S(2)}) async-start(), calls=%async_computation.3 | async-start | bytes 3932160
  800.5 53.4 %copy-start.1 = (bf16[2,24,64,128]{3,2,1,0:T(8,128)(2,1)S(1)}, bf16[2,24,64,128]{3,2,1,0:T(8,128)(2,1)}, u32[]{:S(2)}) copy-start(bf16[2,24,64,128]{3,2,1,0:T(8,128)(2,1)} %param.9) | copy-start | bytes 2359300
Sparse Core Ops, SparseCore 0:
  814.6 37.0 reduce-scatter.4
where the time goes:
time: 862 us; the launch traced here: 861 us
  waiting for transfers between devices  705 us (82%)
  local copies, waits for them, and re-layouts  76 us (9%)
  matrix products  38 us (4%)
  starting transfers between devices  15.9 us (2%)
  between operations  13.5 us (2%)
  other arithmetic  12.4 us (1%)
    all_to_all x1, waiting for transfers between devices, body(): lax.all_to_all(empty.at[slot_of].set(half), 'bond', split_axis=0, concat_...  668 us
    unnamed x2, waiting for transfers between devices  37.3 us
    scatter x1, local copies, waits for them, and re-layouts, body(): empty.at[slot_of].set(half)  35 us
    dot_general x1, matrix products, body(): jnp.einsum('jvwca,wjcd->vjad', received, right_pieces, preferred_element_...  19.6 us
  transfers between devices with their start and end apart: 3, of which 2 were waited for; matrix products, arithmetic and copies ran while one was open for 10% of the time, Pallas kernels for 0%

commit v1 on v0

--- a/solution.py
+++ b/solution.py
@@ -1,10 +1,421 @@
+import functools
+
 import jax
 import jax.numpy as jnp
 from jax import lax
+from jax.experimental import pallas as pl
+from jax.experimental.pallas import tpu as pltpu
 from jax.sharding import PartitionSpec as P
 
+MESH = pl.DeviceIdType.MESH
+MIB = 1024 * 1024
+
+
+def contract_kernel(
+    peers,
+    steps,
+    cap,
+    lsec,
+    dest,
+    rsec,
+    lsize,
+    rsize,
+    slot_src,
+    labels,
+    psi_hbm,
+    left_hbm,
+    right_hbm,
+    landed,
+    lab_out,
+    psi_v,
+    left_v,
+    acc,
+    send_a,
+    recv_a,
+    send_b,
+    recv_b,
+    mine,
+    done,
+    send_c,
+    chunks,
+    psi_sem,
+    left_sem,
+    own_sem,
+    swap_sem,
+    lab_send,
+    lab_recv,
+    lab_own,
+    right_send,
+    left_send,
+    hop_recv,
+    a_sem,
+    b_sem,
+    c_send,
+    c_recv,
+    c_own,
+):
+    me = lax.axis_index("bond")
+    m = lax.axis_index("mpo")
+    s = lax.axis_index("sub")
+    other = {"sub": 1 - s}
+    half_w = left_v.shape[0]
+    wide = half_w // steps
+    width = right_hbm.shape[2]
+    states = right_hbm.shape[3]
+    sectors = right_hbm.shape[1]
+    blocks = psi_v.shape[1]
+    rows = states // 4
+
+    def remote(src, dst, send_sem, recv_sem, where):
+        return pltpu.make_async_remote_copy(
+            src_ref=src,
+            dst_ref=dst,
+            send_sem=send_sem,
+            recv_sem=recv_sem,
+            device_id=where,
+            device_id_type=MESH,
+        )
+
+    left_copy = pltpu.make_async_copy(left_hbm.at[pl.ds(s * half_w, half_w)], left_v, left_sem)
+    left_copy.start()
+    own = []
+    for i in range(steps):
+        cp = pltpu.make_async_copy(
+            right_hbm.at[pl.ds(s * half_w + i * wide, wide)],
+            chunks[i].at[me, :, :, pl.ds(s * width, width)],
+            own_sem.at[i],
+        )
+        cp.start()
+        own.append(cp)
+    psi_own = pltpu.make_async_copy(psi_hbm, psi_v.at[:, :, pl.ds(s * width, width)], psi_sem.at[0])
+    psi_own.start()
+
+    barrier = pltpu.get_barrier_semaphore()
+    pl.semaphore_signal(barrier, inc=1, device_id=other, device_id_type=MESH)
+    pl.semaphore_signal(barrier, inc=1, device_id={"mpo": 1 - m}, device_id_type=MESH)
+    for delta in range(1, peers):
+        pl.semaphore_signal(
+            barrier, inc=1, device_id={"bond": lax.rem(me + delta, peers)}, device_id_type=MESH
+        )
+    pl.semaphore_wait(barrier, peers + 1)
+
+    swaps = []
+    for i in range(steps):
+        cp = remote(
+            right_hbm.at[pl.ds((1 - s) * half_w + i * wide, wide)],
+            chunks[i].at[me, :, :, pl.ds(s * width, width)],
+            swap_sem.at[0, i],
+            swap_sem.at[1, i],
+            other,
+        )
+        cp.start()
+        swaps.append(cp)
+    psi_swap = remote(
+        psi_hbm, psi_v.at[:, :, pl.ds(s * width, width)], psi_sem.at[1], psi_sem.at[2], other
+    )
+    psi_swap.start()
+
+    lane = lax.broadcasted_iota(jnp.int32, (states, states), 1)
+    row = lax.broadcasted_iota(jnp.int32, (states, states), 0)
+
+    def to_right(i, src):
+        return remote(
+            chunks[i].at[src],
+            chunks[i].at[src],
+            right_send.at[i, src],
+            hop_recv.at[i, src],
+            {"bond": lax.rem(me + 1, peers)},
+        )
+
+    def to_left(i, src):
+        return remote(
+            chunks[i].at[src],
+            chunks[i].at[src],
+            left_send.at[i, src],
+            hop_recv.at[i, src],
+            {"bond": lax.rem(me + peers - 1, peers)},
+        )
+
+    for i in range(steps):
+        own[i].wait()
+        swaps[i].wait_recv()
+
+        @pl.loop(0, sectors)
+        def _(r):
+            keep = jnp.where((lane < rsize[r]) & (row < rsize[r]), 1.0, 0.0).astype(jnp.bfloat16)
+            for w in range(wide):
+                chunks[i][me, w, r] = chunks[i][me, w, r] * keep
+
+        @pl.when(me < peers - 1)
+        def _():
+            to_right(i, me).start()
+
+        @pl.when(me > 0)
+        def _():
+            to_left(i, me).start()
+
+    lab_copies = []
+    for delta in range(1, peers):
+        q = lax.rem(me + delta, peers)
+        cp = remote(labels.at[q], lab_out.at[me], lab_send.at[q], lab_recv.at[me], {"bond": q})
+        cp.start()
+        lab_copies.append(cp)
+    lab_mine = pltpu.make_async_copy(labels.at[me], lab_out.at[me], lab_own)
+    lab_mine.start()
+
+    psi_own.wait()
+    psi_swap.wait()
+    left_copy.wait()
+
+    def forward(h, i):
+        @pl.when(me - h >= 0)
+        def _():
+            to_right(i, me - h).wait_recv()
+
+            @pl.when(me < peers - 1)
+            def _():
+                to_right(i, me - h).start()
+
+        @pl.when(me + h <= peers - 1)
+        def _():
+            to_left(i, me + h).wait_recv()
+
+            @pl.when(me > 0)
+            def _():
+                to_left(i, me + h).start()
+
+    def compute(i):
+        @pl.loop(0, blocks)
+        def _(k):
+            l = lsec[k]
+            q = dest[k]
+            r = rsec[k]
+            keep = jnp.where(lane < lsize[l], 1.0, 0.0).astype(jnp.bfloat16)
+            vec = jnp.concatenate([psi_v[0, k] * keep, psi_v[1, k] * keep], axis=0)
+            tops, bottoms, pieces = [], [], []
+            for w in range(wide):
+                out = lax.dot_general(
+                    left_v[i * wide + w, l],
+                    vec,
+                    (((1,), (1,)), ((), ())),
+                    preferred_element_type=jnp.float32,
+                ).astype(jnp.bfloat16)
+                tops.append(out[:, :states])
+                bottoms.append(out[:, states:])
+                pieces.append(chunks[i][q, w, r])
+            lhs = jnp.concatenate(
+                [jnp.concatenate(tops, axis=1), jnp.concatenate(bottoms, axis=1)], axis=0
+            )
+            rhs = jnp.concatenate(pieces, axis=0)
+            total = jnp.dot(lhs, rhs, preferred_element_type=jnp.float32)
+            if i == 0:
+                acc[k] = total
+            else:
+                acc[k] += total
+
+    for h in range(1, peers - 1):
+        for i in range(steps):
+            forward(h, i)
+    for i in range(steps):
+        forward(peers - 1, i)
+        compute(i)
+
+    piece_row = lax.broadcasted_iota(jnp.int32, (rows, states), 0)
+
+    def piece(k, v, mm, ss):
+        start = mm * (2 * rows) + ss * rows
+        value = acc[k, pl.ds(pl.multiple_of(v * states + start, rows), rows)]
+        return jnp.where(piece_row + start < lsize[lsec[k]], value, 0.0)
+
+    @pl.loop(0, blocks)
+    def _(k):
+        for v in range(2):
+            for mm in range(2):
+                send_a[k, v, mm] = piece(k, v, mm, 1 - s).astype(jnp.bfloat16)
+
+    copy_a = remote(send_a, recv_a, a_sem.at[0], a_sem.at[1], other)
+    copy_a.start()
+    copy_a.wait()
+
+    @pl.loop(0, blocks)
+    def _(k):
+        for v in range(2):
+            send_b[k, v] = (
+                piece(k, v, 1 - m, s) + recv_a[k, v, 1 - m].astype(jnp.float32)
+            ).astype(jnp.bfloat16)
+
+    copy_b = remote(send_b, recv_b, b_sem.at[0], b_sem.at[1], {"mpo": 1 - m})
+    copy_b.start()
+
+    @pl.loop(0, blocks)
+    def _(k):
+        for v in range(2):
+            mine[k, v] = piece(k, v, m, s) + recv_a[k, v, m].astype(jnp.float32)
+
+    copy_b.wait()
+
+    @pl.loop(0, blocks)
+    def _(k):
+        for v in range(2):
+            done[k, v] = (mine[k, v] + recv_b[k, v].astype(jnp.float32)).astype(jnp.bfloat16)
+
+    c_copies = []
+    for delta in range(1, peers + 1):
+        q = lax.rem(me + delta, peers)
+
+        @pl.loop(0, cap)
+        def _(j):
+            send_c[q, j] = done[slot_src[q * cap + j]]
+
+        if delta < peers:
+            cp = remote(send_c.at[q], landed.at[me], c_send.at[q], c_recv.at[me], {"bond": q})
+        else:
+            cp = pltpu.make_async_copy(send_c.at[me], landed.at[me], c_own)
+        cp.start()
+        c_copies.append(cp)
+
+    for delta in range(1, peers):
+        c_copies[delta - 1].wait_send()
+        src = lax.rem(me + peers - delta, peers)
+        remote(
+            send_c.at[src], landed.at[src], c_send.at[src], c_recv.at[src], {"bond": src}
+        ).wait_recv()
+        lab_copies[delta - 1].wait_send()
+        remote(
+            labels.at[src], lab_out.at[src], lab_send.at[src], lab_recv.at[src], {"bond": src}
+        ).wait_recv()
+    c_copies[-1].wait()
+    lab_mine.wait()
+    for i in range(steps):
+        swaps[i].wait_send()
+        for h in range(peers):
+
+            @pl.when((me - h >= 0) & (me < peers - 1))
+            def _():
+                to_right(i, me - h).wait_send()
+
+            @pl.when((me + h <= peers - 1) & (me > 0))
+            def _():
+                to_left(i, me + h).wait_send()
+
+
+def add_kernel(peers, cap, labels, landed, out, total):
+    total[...] = jnp.zeros_like(total)
+    for p in range(peers):
+
+        @pl.loop(0, cap)
+        def _(j):
+            t = labels[p, 0, j]
+
+            @pl.when(t >= 0)
+            def _():
+                total[t] += landed[p, j].astype(jnp.float32)
+
+    for v in range(2):
+        out[v] = total[:, v].astype(out.dtype)
+
 
 def body(
+    psi,
+    left_env,
+    right_env,
+    left_sector,
+    right_sector,
+    dest_device,
+    target_block,
+    left_size,
+    right_size,
+):
+    blocks = psi.shape[1]
+    width = psi.shape[2]
+    states = psi.shape[3]
+    sectors = right_env.shape[1]
+    half_w = right_env.shape[0] // 2
+    peers = lax.axis_size("bond")
+    cap = max(2, 2 * blocks // peers)
+    steps = 5
+    wide = half_w // steps
+    rows = states // 4
+    destination = dest_device[:, 0]
+    hits = destination[:, None] == jnp.arange(peers, dtype=jnp.int32)[None, :]
+    before = jnp.arange(blocks)[None, :] < jnp.arange(blocks)[:, None]
+    same = destination[None, :] == destination[:, None]
+    rank = jnp.sum((before & same).astype(jnp.int32), axis=1)
+    at = hits[:, :, None] & (rank[:, None, None] == jnp.arange(128, dtype=jnp.int32)[None, None, :])
+    ids = jnp.arange(blocks, dtype=jnp.int32)
+    slot_src = jnp.sum(jnp.where(at, ids[:, None, None], 0), axis=0)[:, :cap].reshape(-1)
+    lab = jnp.sum(jnp.where(at, target_block[:, None, None] + 1, 0), axis=0) - 1
+    labels = jnp.broadcast_to(lab[:, None, :], (peers, 8, 128)).astype(jnp.int32)
+
+    smem = pl.BlockSpec(memory_space=pltpu.SMEM)
+    vmem = pl.BlockSpec(memory_space=pltpu.VMEM)
+    hbm = pl.BlockSpec(memory_space=pl.ANY)
+    bf16, f32 = jnp.bfloat16, jnp.float32
+    dma = pltpu.SemaphoreType.DMA
+    landed, lab_in = pl.pallas_call(
+        functools.partial(contract_kernel, peers, steps, cap),
+        out_shape=(
+            jax.ShapeDtypeStruct((peers, cap, 2, rows, states), bf16),
+            jax.ShapeDtypeStruct((peers, 8, 128), jnp.int32),
+        ),
+        in_specs=[smem] * 6 + [vmem] + [hbm] * 3,
+        out_specs=(hbm, hbm),
+        scratch_shapes=[
+            pltpu.VMEM((2, blocks, states, states), bf16),
+            pltpu.VMEM((half_w, sectors, states, states), bf16),
+            pltpu.VMEM((blocks, 2 * states, states), f32),
+            pltpu.VMEM((blocks, 2, 2, rows, states), bf16),
+            pltpu.VMEM((blocks, 2, 2, rows, states), bf16),
+            pltpu.VMEM((blocks, 2, rows, states), bf16),
+            pltpu.VMEM((blocks, 2, rows, states), bf16),
+            pltpu.VMEM((blocks, 2, rows, states), f32),
+            pltpu.VMEM((blocks, 2, rows, states), bf16),
+            pltpu.VMEM((peers, cap, 2, rows, states), bf16),
+            [pltpu.VMEM((peers, wide, sectors, states, states), bf16) for _ in range(steps)],
+            dma((3,)),
+            dma,
+            dma((steps,)),
+            dma((2, steps)),
+            dma((peers,)),
+            dma((peers,)),
+            dma,
+            dma((steps, peers)),
+            dma((steps, peers)),
+            dma((steps, peers)),
+            dma((2,)),
+            dma((2,)),
+            dma((peers,)),
+            dma((peers,)),
+            dma,
+        ],
+        compiler_params=pltpu.CompilerParams(
+            collective_id=0, has_side_effects=True, vmem_limit_bytes=60 * MIB
+        ),
+        name="gather_contract",
+    )(
+        left_sector,
+        destination,
+        right_sector,
+        left_size,
+        right_size,
+        slot_src,
+        labels,
+        psi,
+        left_env,
+        right_env,
+    )
+    return pl.pallas_call(
+        functools.partial(add_kernel, peers, cap),
+        out_shape=jax.ShapeDtypeStruct((2, blocks, rows, states), bf16),
+        in_specs=[smem, vmem],
+        out_specs=vmem,
+        scratch_shapes=[pltpu.VMEM((blocks, 2, rows, states), f32)],
+        compiler_params=pltpu.CompilerParams(vmem_limit_bytes=32 * MIB),
+        name="add_targets",
+    )(lab_in, landed)
+
+
+def plain_body(
     psi,
     left_env,
     right_env,
@@ -79,4 +490,5 @@
         P(("grp", "bond")),
     )
     out_specs = P(None, ("grp", "bond"), ("mpo", "sub"), None)
-    return jax.shard_map(body, mesh=mesh, in_specs=in_specs, out_specs=out_specs, check_vma=False)
+    paired = mesh.shape["mpo"] == 2 and mesh.shape["sub"] == 2
+    return jax.shard_map(body if paired else plain_body, mesh=mesh, in_specs=in_specs, out_specs=out_specs, check_vma=False)

time: 862 us -> 223 us (0.26)
  waiting for transfers between devices: 705 us -> 0 us
  Pallas kernels: 0 us -> 217 us
  local copies, waits for them, and re-layouts: 76 us -> 3.02 us
  matrix products: 38 us -> 0 us
  starting transfers between devices: 15.9 us -> 0 us
  between operations: 13.5 us -> 0.03 us
  other arithmetic: 12.4 us -> 2.41 us
    all_to_all x2 -> x0, waiting for transfers between devices: 668 us -> none  [the longest x1 668 us: body(): lax.all_to_all(empty.at[slot_of].set(half), 'bond', split_axis=0, concat_...]
    pallas_call x0 -> x2, Pallas kernels: none -> 217 us  [the longest x1 214 us: body(): pl.pallas_call(functools.partial(contract_kernel, peers, steps, cap), out...]
    dot_general x3 -> x0, matrix products: 38 us -> none  [the longest x1 19.6 us: body(): jnp.einsum('jvwca,wjcd->vjad', received, right_pieces, preferred_element_...]
    unnamed x2 -> x0, waiting for transfers between devices: 37.3 us -> none
    scatter x3 -> x0, local copies, waits for them, and re-layouts: 35.7 us -> none  [the longest x1 35 us: body(): empty.at[slot_of].set(half)]
    gather x2 -> x0, local copies, waits for them, and re-layouts: 17.1 us -> none  [the longest x1 9.72 us: body(): left_pieces = masked_left[:, left_sector]]
    all_to_all x2 -> x0, starting transfers between devices: 15.8 us -> none  [the longest x1 9.52 us: body(): lax.all_to_all(empty.at[slot_of].set(half), 'bond', split_axis=0, concat_...]
    broadcast_in_dim x1, local copies, waits for them, and re-layouts: 10.6 us -> 0.61 us  [body(): jnp.broadcast_to(lab[:, None, :], (peers, 8, 128)).astype(jnp.int32)]
  transfers between devices with their start and end apart: 3 -> 0, of which waited for: 2 -> 0; matrix products, arithmetic and copies ran while one was open for 10% -> 0% of each run, Pallas kernels for 0% -> 0%
where the time goes in v1:
time: 223 us; the launch traced here: 222 us
  Pallas kernels  217 us (97%)
  local copies, waits for them, and re-layouts  3.02 us (1%)
  other arithmetic  2.41 us (1%)
    pallas_call x1, Pallas kernels, body(): pl.pallas_call(functools.partial(contract_kernel, peers, steps, cap), out...  214 us

profile of v1, /device:TPU:0, one launch (start us, length us, event | category | flops | bytes accessed | tf_op | source)
XLA Modules:
  0.0 222.3 jit_solution(16498961764202413006)
XLA Ops:
  0.0 0.9 convert_reduce_fusion
  0.9 0.7 iota_compare_fusion.2
  1.6 0.7 broadcast_add_fusion.1
  2.2 0.1 iota_compare_fusion
  2.3 0.1 fusion.1
  2.4 0.6 reshape.52.slot_src
  3.0 0.6 broadcast_in_dim.35.labels
  3.6 214.5 %gather_contract.1 = (bf16[4,12,2,32,128]{4,3,2,1,0:T(8,128)(2,1)}, s32[4,8,128]{2,1,0:T(8,128)}) custom-call(s32[24]{0:T(128)} %lsec.1, s32[24]{0:T(128)} %bitcast.5, s32[24]{0:T(128)} %rsec.1, s32[8]{0:T(128)} %lsize.1, s32[8]{0:T(128)} %rsize.1, s32[48]{0:T(128)} %reshape.52.slot_src, s32[4,8,128]{2,1,0:T(8,128)} %broadcast_in_dim.35.labels, ...), custom_call_target="tpu_custom_call" | custom-call | tf_op jit(solution)/shard_map/gather_contract/pallas_call | solution.py:355
  218.1 0.0 copy-start
  218.1 1.1 copy-done
  219.2 0.0 copy-start.1
  219.2 0.7 copy-done.1
  219.9 2.4 %add_targets.1 = bf16[2,24,32,128]{3,2,1,0:T(8,128)(2,1)} custom-call(s32[4,8,128]{2,1,0:T(8,128)S(1)} %copy-done.1, bf16[4,12,2,32,128]{4,3,2,1,0:T(8,128)(2,1)S(1)} %copy-done), custom_call_target="tpu_custom_call" | custom-call | tf_op jit(solution)/shard_map/add_targets/pallas_call | solution.py:407
  (1 shorter events, 0.0 us)
Async XLA Ops:
  218.1 1.1 copy-start
  219.2 0.7 copy-start.1

commit v2 on v1

--- a/solution.py
+++ b/solution.py
@@ -9,17 +9,22 @@
 
 MESH = pl.DeviceIdType.MESH
 MIB = 1024 * 1024
+UNROLL = 2
+LEVELS = (20, 23, 26)
 
 
 def contract_kernel(
     peers,
     steps,
     cap,
+    groups,
     lsec,
     dest,
-    rsec,
+    offset,
     lsize,
     rsize,
+    order,
+    order_size,
     slot_src,
     labels,
     psi_hbm,
@@ -37,6 +42,7 @@
     mine,
     done,
     send_c,
+    stage,
     chunks,
     psi_sem,
     left_sem,
@@ -60,9 +66,10 @@
     other = {"sub": 1 - s}
     half_w = left_v.shape[0]
     wide = half_w // steps
-    width = right_hbm.shape[2]
-    states = right_hbm.shape[3]
-    sectors = right_hbm.shape[1]
+    width = psi_hbm.shape[2]
+    states = psi_hbm.shape[3]
+    parts = right_hbm.shape[2]
+    spare = chunks[0].shape[2] - groups
     blocks = psi_v.shape[1]
     rows = states // 4
 
@@ -82,7 +89,7 @@
     for i in range(steps):
         cp = pltpu.make_async_copy(
             right_hbm.at[pl.ds(s * half_w + i * wide, wide)],
-            chunks[i].at[me, :, :, pl.ds(s * width, width)],
+            stage[i].at[:, :, pl.ds(s * parts, parts)],
             own_sem.at[i],
         )
         cp.start()
@@ -103,7 +110,7 @@
     for i in range(steps):
         cp = remote(
             right_hbm.at[pl.ds((1 - s) * half_w + i * wide, wide)],
-            chunks[i].at[me, :, :, pl.ds(s * width, width)],
+            stage[i].at[:, :, pl.ds(s * parts, parts)],
             swap_sem.at[0, i],
             swap_sem.at[1, i],
             other,
@@ -120,8 +127,8 @@
 
     def to_right(i, src):
         return remote(
-            chunks[i].at[src],
-            chunks[i].at[src],
+            chunks[i].at[src, :, pl.ds(0, groups)],
+            chunks[i].at[src, :, pl.ds(0, groups)],
             right_send.at[i, src],
             hop_recv.at[i, src],
             {"bond": lax.rem(me + 1, peers)},
@@ -129,8 +136,8 @@
 
     def to_left(i, src):
         return remote(
-            chunks[i].at[src],
-            chunks[i].at[src],
+            chunks[i].at[src, :, pl.ds(0, groups)],
+            chunks[i].at[src, :, pl.ds(0, groups)],
             left_send.at[i, src],
             hop_recv.at[i, src],
             {"bond": lax.rem(me + peers - 1, peers)},
@@ -140,11 +147,13 @@
         own[i].wait()
         swaps[i].wait_recv()
 
-        @pl.loop(0, sectors)
-        def _(r):
-            keep = jnp.where((lane < rsize[r]) & (row < rsize[r]), 1.0, 0.0).astype(jnp.bfloat16)
+        @pl.loop(0, groups, unroll=4)
+        def _(g):
+            keep = jnp.where(lane[:16] < order_size[g], 1.0, 0.0).astype(jnp.bfloat16)
+            r = order[g] // (2 * parts)
+            part = order[g] % (2 * parts)
             for w in range(wide):
-                chunks[i][me, w, r] = chunks[i][me, w, r] * keep
+                chunks[i][me, w, g] = stage[i][w, r, part] * keep
 
         @pl.when(me < peers - 1)
         def _():
@@ -163,6 +172,10 @@
     lab_mine = pltpu.make_async_copy(labels.at[me], lab_out.at[me], lab_own)
     lab_mine.start()
 
+    for i in range(steps):
+        for p in range(peers):
+            chunks[i][p, :, groups:] = jnp.zeros((wide, spare) + chunks[i].shape[3:], jnp.bfloat16)
+
     psi_own.wait()
     psi_swap.wait()
     left_copy.wait()
@@ -185,12 +198,13 @@
                 to_left(i, me + h).start()
 
     def compute(i):
-        @pl.loop(0, blocks)
+        @pl.loop(0, blocks, unroll=UNROLL)
         def _(k):
             l = lsec[k]
             q = dest[k]
-            r = rsec[k]
-            keep = jnp.where(lane < lsize[l], 1.0, 0.0).astype(jnp.bfloat16)
+            start = offset[k]
+            inside = (lane < lsize[l]) & (row < rsize[k])
+            keep = jnp.where(inside, 1.0, 0.0).astype(jnp.bfloat16)
             vec = jnp.concatenate([psi_v[0, k] * keep, psi_v[1, k] * keep], axis=0)
             tops, bottoms, pieces = [], [], []
             for w in range(wide):
@@ -202,7 +216,9 @@
                 ).astype(jnp.bfloat16)
                 tops.append(out[:, :states])
                 bottoms.append(out[:, states:])
-                pieces.append(chunks[i][q, w, r])
+                pieces.append(
+                    chunks[i][q, w, pl.ds(start, 2 * parts)].reshape(states, states)
+                )
             lhs = jnp.concatenate(
                 [jnp.concatenate(tops, axis=1), jnp.concatenate(bottoms, axis=1)], axis=0
             )
@@ -347,62 +363,98 @@
     lab = jnp.sum(jnp.where(at, target_block[:, None, None] + 1, 0), axis=0) - 1
     labels = jnp.broadcast_to(lab[:, None, :], (peers, 8, 128)).astype(jnp.int32)
 
+    group = 16
+    per = states // group
+    total_groups = sectors * per
+    sizes = lax.all_gather(right_size, ("grp", "bond"), axis=0, tiled=True).reshape(-1, sectors)
+    counts = (sizes + (group - 1)) // group
+    need = jnp.max(jnp.sum(counts, axis=1))
+    low = jnp.tril(jnp.ones((sectors, sectors), jnp.int32), -1)
+    starts = jnp.sum(counts[:, None, :] * low[None], axis=2)
+    part = lax.axis_index("grp")
+    sizes_here = lax.dynamic_slice_in_dim(sizes, part * peers, peers, 0)
+    starts_here = lax.dynamic_slice_in_dim(starts, part * peers, peers, 0)
+    named = (destination * sectors + right_sector)[:, None] == jnp.arange(peers * sectors)[None, :]
+    offset = jnp.sum(jnp.where(named, starts_here.reshape(1, -1), 0), axis=1)
+    rsize = jnp.sum(jnp.where(named, sizes_here.reshape(1, -1), 0), axis=1)
+    own_counts = (right_size + (group - 1)) // group
+    own_starts = jnp.sum(own_counts[None, :] * low, axis=1)
+    each = jnp.arange(total_groups, dtype=jnp.int32).reshape(sectors, per)
+    inner = jnp.arange(per, dtype=jnp.int32)[None, :]
+    place = jnp.where(inner < own_counts[:, None], own_starts[:, None] + inner, -1)
+    fits = place[None] == jnp.arange(total_groups, dtype=jnp.int32)[:, None, None]
+    order = jnp.sum(jnp.where(fits, each[None], 0), axis=(1, 2))
+    order_size = jnp.sum(jnp.where(fits, right_size[None, :, None], 0), axis=(1, 2))
+    levels = [total_groups * f // 32 for f in LEVELS] + [total_groups]
+    level = sum((need > at).astype(jnp.int32) for at in levels[:-1])
+
     smem = pl.BlockSpec(memory_space=pltpu.SMEM)
     vmem = pl.BlockSpec(memory_space=pltpu.VMEM)
     hbm = pl.BlockSpec(memory_space=pl.ANY)
     bf16, f32 = jnp.bfloat16, jnp.float32
     dma = pltpu.SemaphoreType.DMA
-    landed, lab_in = pl.pallas_call(
-        functools.partial(contract_kernel, peers, steps, cap),
-        out_shape=(
-            jax.ShapeDtypeStruct((peers, cap, 2, rows, states), bf16),
-            jax.ShapeDtypeStruct((peers, 8, 128), jnp.int32),
-        ),
-        in_specs=[smem] * 6 + [vmem] + [hbm] * 3,
-        out_specs=(hbm, hbm),
-        scratch_shapes=[
-            pltpu.VMEM((2, blocks, states, states), bf16),
-            pltpu.VMEM((half_w, sectors, states, states), bf16),
-            pltpu.VMEM((blocks, 2 * states, states), f32),
-            pltpu.VMEM((blocks, 2, 2, rows, states), bf16),
-            pltpu.VMEM((blocks, 2, 2, rows, states), bf16),
-            pltpu.VMEM((blocks, 2, rows, states), bf16),
-            pltpu.VMEM((blocks, 2, rows, states), bf16),
-            pltpu.VMEM((blocks, 2, rows, states), f32),
-            pltpu.VMEM((blocks, 2, rows, states), bf16),
-            pltpu.VMEM((peers, cap, 2, rows, states), bf16),
-            [pltpu.VMEM((peers, wide, sectors, states, states), bf16) for _ in range(steps)],
-            dma((3,)),
-            dma,
-            dma((steps,)),
-            dma((2, steps)),
-            dma((peers,)),
-            dma((peers,)),
-            dma,
-            dma((steps, peers)),
-            dma((steps, peers)),
-            dma((steps, peers)),
-            dma((2,)),
-            dma((2,)),
-            dma((peers,)),
-            dma((peers,)),
-            dma,
-        ],
-        compiler_params=pltpu.CompilerParams(
-            collective_id=0, has_side_effects=True, vmem_limit_bytes=60 * MIB
-        ),
-        name="gather_contract",
-    )(
+    def contract(number, groups, *operands):
+        return pl.pallas_call(
+            functools.partial(contract_kernel, peers, steps, cap, groups),
+            out_shape=(
+                jax.ShapeDtypeStruct((peers, cap, 2, rows, states), bf16),
+                jax.ShapeDtypeStruct((peers, 8, 128), jnp.int32),
+            ),
+            in_specs=[smem] * 8 + [vmem] + [hbm] * 3,
+            out_specs=(hbm, hbm),
+            scratch_shapes=[
+                pltpu.VMEM((2, blocks, states, states), bf16),
+                pltpu.VMEM((half_w, sectors, states, states), bf16),
+                pltpu.VMEM((blocks, 2 * states, states), f32),
+                pltpu.VMEM((blocks, 2, 2, rows, states), bf16),
+                pltpu.VMEM((blocks, 2, 2, rows, states), bf16),
+                pltpu.VMEM((blocks, 2, rows, states), bf16),
+                pltpu.VMEM((blocks, 2, rows, states), bf16),
+                pltpu.VMEM((blocks, 2, rows, states), f32),
+                pltpu.VMEM((blocks, 2, rows, states), bf16),
+                pltpu.VMEM((peers, cap, 2, rows, states), bf16),
+                [pltpu.VMEM((wide, sectors, per, group, states), bf16) for _ in range(steps)],
+                [
+                    pltpu.VMEM((peers, wide, groups + per, group, states), bf16)
+                    for _ in range(steps)
+                ],
+                dma((3,)),
+                dma,
+                dma((steps,)),
+                dma((2, steps)),
+                dma((peers,)),
+                dma((peers,)),
+                dma,
+                dma((steps, peers)),
+                dma((steps, peers)),
+                dma((steps, peers)),
+                dma((2,)),
+                dma((2,)),
+                dma((peers,)),
+                dma((peers,)),
+                dma,
+            ],
+            compiler_params=pltpu.CompilerParams(
+                collective_id=number, has_side_effects=True, vmem_limit_bytes=60 * MIB
+            ),
+            name="gather_contract_%d" % groups,
+        )(*operands)
+
+    landed, lab_in = lax.switch(
+        level,
+        [functools.partial(contract, i, groups) for i, groups in enumerate(levels)],
         left_sector,
         destination,
-        right_sector,
+        offset,
         left_size,
-        right_size,
+        rsize,
+        order,
+        order_size,
         slot_src,
         labels,
         psi,
         left_env,
-        right_env,
+        right_env.reshape(right_env.shape[:2] + (width // group, group, states)),
     )
     return pl.pallas_call(
         functools.partial(add_kernel, peers, cap),

time: 223 us -> 187 us (0.84)
  Pallas kernels: 217 us -> 163 us
  blocking collectives: 0 us -> 13 us
  other arithmetic: 2.41 us -> 5.94 us
  between operations: 0.03 us -> 2.65 us
    pallas_call x1, Pallas kernels: 214 us -> 161 us  [contract(): pl.pallas_call(functools.partial(contract_kernel, peers, steps, cap, grou...]
    unnamed x0 -> x1, blocking collectives: none -> 13 us
where the time goes in v2:
time: 187 us
  Pallas kernels  163 us (87%)
  blocking collectives  13 us (7%)
  other arithmetic  5.94 us (3%)
  between operations  2.65 us (1%)
  local copies, waits for them, and re-layouts  2.41 us (1%)
    pallas_call x1, Pallas kernels, contract(): pl.pallas_call(functools.partial(contract_kernel, peers, steps, cap, grou...  161 us
    unnamed x1, blocking collectives  13 us

profile of v2, /device:TPU:0, one launch (start us, length us, event | category | flops | bytes accessed | tf_op | source)
XLA Modules:
  0.0 187.0 jit_solution(15681806245832430587)
XLA Ops:
  0.0 1.2 dynamic-slice
  1.9 0.7 and_select_fusion.2
  2.6 0.7 multiply_add_fusion.1
  3.2 0.7 broadcast_add_fusion.1
  3.9 0.9 convert_reduce_fusion
  4.8 0.7 iota_compare_fusion.6
  5.5 0.8 dynamic-update-slice
  6.3 13.0 %all-reduce = s32[64]{0:T(128)S(1)} all-reduce(s32[64]{0:T(128)S(1)} %dynamic-update-slice), channel_id=1, replica_groups=mesh['grp'=2,'bond'=4,'mpo'=2,'sub'=2] {'grp','bond'}, use_global_device_ids=true, to_apply=%add | all-reduce | flops 64 | bytes 512
  19.3 0.1 iota_compare_fusion.1
  19.4 0.1 fusion.1
  19.5 0.1 reshape.147
  19.6 0.1 reshape.146
  19.7 0.2 multiply_reduce_fusion.1
  19.8 0.1 add_select_fusion.1
  19.9 0.8 select_reduce_fusion
  20.7 0.1 fusion.6
  20.8 0.6 reduce_max.9
  23.4 0.2 multiply_reduce_fusion
  23.6 0.1 broadcast_in_dim.95
  23.7 0.1 broadcast_in_dim.92
  23.8 0.2 select_reduce_fusion.2
  24.0 160.6 %conditional.1 = ((bf16[4,12,2,32,128]{4,3,2,1,0:T(8,128)(2,1)S(1)}, s32[4,8,128]{2,1,0:T(8,128)S(1)})) conditional(s32[]{:T(128)} %clamp.3, (s32[24]{0:T(128)}, s32[24]{0:T(128)}, s32[24]{0:T(128)S(1)}, s32[8]{0:T(128)}, s32[24]{0:T(128)S(1)}, /*index=5*/s32[64]{0:T(128)S(1)}, s32[64]{0:T(128)S(1)}, ...), branch_computations={%region_11.12_spmd, %region_12.13_spmd, %region_13.14_spmd, %regio... | conditional | bytes 8 | solution.py:443
  24.0 160.5 %gather_contract_46.1 = (bf16[4,12,2,32,128]{4,3,2,1,0:T(8,128)(2,1)S(1)}, s32[4,8,128]{2,1,0:T(8,128)S(1)}) custom-call(s32[24]{0:T(128)} %get-tuple-element.113.lsec, s32[24]{0:T(128)} %get-tuple-element.114.dest, s32[24]{0:T(128)S(1)} %get-tuple-element.115.offset, s32[8]{0:T(128)} %get-tuple-element.116.lsize, s32[24]{0:T(128)S(1)} %get-tuple-element.117.rsize, ...), custom_call_target="tpu_custom_call" | custom-call | tf_op jit(solution)/shard_map/cond/branch_1_fun/gather_contract_46/pallas_call | solution.py:397
  184.6 2.4 %add_targets.1 = bf16[2,24,32,128]{3,2,1,0:T(8,128)(2,1)} custom-call(s32[4,8,128]{2,1,0:T(8,128)S(1)} %get-tuple-element.151.labels, bf16[4,12,2,32,128]{4,3,2,1,0:T(8,128)(2,1)S(1)} %get-tuple-element.152.landed), custom_call_target="tpu_custom_call" | custom-call | tf_op jit(solution)/shard_map/add_targets/pallas_call | solution.py:459
  (6 shorter events, 0.0 us)
